TPU v7x, 32 devices: a whole 2x2x4 slice. The times are simulated.
32 devices in a mesh: visit: 8 (over y, x, core), sky: 4 (over z).
Axes of the slice: x: 2, y: 2, z: 4, core: 2. Of those that a mesh axis runs over, the one named last changes fastest.
Arguments:
- image: bfloat16 [8, 384, 2048], P('visit', None, 'sky'), may hold values from -16 to 16
- variance: bfloat16 [8, 384, 2048], P('visit', None, 'sky'), may hold values from 0.25 to 4
- mask_bits: int32 [8, 384, 2048], P('visit', None, 'sky'), may hold values from 0 to 63, as said below
- boxes: int32 [8, 4], P('visit'), may hold values from 0 to 2048, as said below
- row_filters: bfloat16 [20, 41], replicated, may hold values from -1 to 1
- col_filters: bfloat16 [20, 41], replicated, may hold values from -1 to 1
- coeffs: float32 [8, 20, 6], P('visit'), may hold values from -1.25 to 1.25
Outputs:
- coadd: float32 [384, 2048], P('visit', 'sky')
- weight_sum: float32 [384, 2048], P('visit', 'sky')
Inputs may be any that keep to these rules, and one draw needn't show every extreme that they name: `mask_bits`: bits 0 to 5 may be set; bits 0, 1 and 2 reject a pixel. `boxes`: for every piece the first row is below the end row and the first column below the end column.
All inputs are finite; a program needn't handle non-finite values.
Results may differ from a plain program's by a relative error of at most 0.0029.
Values may be sent and summed in bfloat16 or wider, within the bound.
A program may use at most 64 MiB of HBM per device.

v0:
```python
import jax
import jax.numpy as jnp
from jax import lax
from jax.sharding import PartitionSpec as P

RAD = 20
ROWS_DEV = 48


reject_bits = 7


def extended_2(shard, sides, width):
    for axis, dim in sides:
        devices, length = (lax.axis_size(axis), shard.shape[dim])
        up = [(i, (i + 1) % devices) for i in range(devices - 1)]
        down = [(j, i) for i, j in up]
        last = lax.slice_in_dim(shard, length - width, length, axis=dim)
        leading = lax.slice_in_dim(shard, 0, width, axis=dim)
        before = lax.ppermute(last, axis, up)
        after = lax.ppermute(leading, axis, down)
        shard = jnp.concatenate([before, shard, after], axis=dim)
    return shard


def toeplitz_stack(filters, out_len, in_len):
    offsets = (
        jnp.arange(in_len, dtype=jnp.int32)[None, :] - jnp.arange(out_len, dtype=jnp.int32)[:, None]
    )
    onehot = (
        offsets[:, :, None] == jnp.arange(filters.shape[1], dtype=jnp.int32)[None, None, :]
    ).astype(jnp.float32)
    return jnp.einsum(
        "oit,bt->boi", onehot, filters.astype(jnp.float32), precision=lax.Precision.HIGHEST
    ).astype(jnp.bfloat16)


def column_windows(padded, col_block, margin):
    count_blocks = (padded.shape[-1] - 2 * margin) // col_block
    return jnp.stack(
        [
            padded[..., block_id * col_block : block_id * col_block + col_block + 2 * margin]
            for block_id in range(count_blocks)
        ],
        axis=-2,
    )


def masked_planes(variance, mask_bits, boxes, col_first):
    row_index = jnp.arange(variance.shape[1], dtype=jnp.int32)[None, :, None]
    col_index = (col_first + jnp.arange(variance.shape[2], dtype=jnp.int32))[None, None, :]
    inside = (row_index >= boxes[:, 0, None, None]) & (row_index < boxes[:, 1, None, None])
    inside = inside & (col_index >= boxes[:, 2, None, None]) & (col_index < boxes[:, 3, None, None])
    inside = inside & (jnp.bitwise_and(mask_bits, reject_bits) == 0)
    return jnp.where(inside, variance, jnp.zeros_like(variance))


def inverse_weight(masked):
    positive = masked > 0
    return jnp.where(
        positive,
        1.0 / jnp.where(positive, masked, jnp.ones_like(masked)).astype(jnp.float32),
        jnp.float32(0.0),
    )


def poly_field(factors, xcoord, ycoord):
    return (
        factors[0]
        + factors[1] * xcoord
        + factors[2] * ycoord
        + factors[3] * (xcoord * xcoord)
        + factors[4] * (xcoord * ycoord)
        + factors[5] * (ycoord * ycoord)
    )


def match_rows(slab_windows, factors, count, col_first, height, width, row_mats, col_mats):
    band_rows = row_mats.shape[1]
    window_rows = row_mats.shape[2]
    col_block = col_mats.shape[1]
    count_blocks = slab_windows.shape[1]
    band_count = count // band_rows
    local_firsts = band_rows * jnp.arange(band_count, dtype=jnp.int32)
    row_pos = jnp.arange(count, dtype=jnp.int32).astype(jnp.float32)
    ycoord = ((2.0 * row_pos + 1.0) / height - 1.0).reshape(band_count, band_rows, 1, 1)
    col_pos = (col_first + jnp.arange(count_blocks * col_block, dtype=jnp.int32)).astype(
        jnp.float32
    )
    xcoord = ((2.0 * col_pos + 1.0) / width - 1.0).reshape(1, 1, count_blocks, col_block)

    def basis_step(total, items):
        col_mat, row_mat, poly_terms = items
        colpass = jnp.einsum(
            "rkj,cj->rkc", slab_windows, col_mat, preferred_element_type=jnp.float32
        ).astype(jnp.bfloat16)
        bands = jax.vmap(
            lambda first_row: lax.dynamic_slice_in_dim(colpass, first_row, window_rows, 0)
        )(local_firsts)
        rowpass = jnp.einsum("sr,nrkc->nskc", row_mat, bands, preferred_element_type=jnp.float32)
        return (total + poly_field(poly_terms, xcoord, ycoord) * rowpass, None)

    start_total = jnp.zeros((band_count, band_rows, count_blocks, col_block), jnp.float32)
    total, _ = lax.scan(basis_step, start_total, (col_mats, row_mats, factors))
    return total.reshape(count, count_blocks * col_block)


def per_device(image, variance, mask_bits, boxes, row_filters, col_filters, coeffs):
    pieces_here, height, cols_here = image.shape
    width = cols_here * lax.axis_size("sky")
    col_first = lax.axis_index("sky") * cols_here
    col_block = min(128, cols_here)
    window_rows = ROWS_DEV + 2 * RAD
    row_mats = toeplitz_stack(row_filters, ROWS_DEV, window_rows)
    col_mats = toeplitz_stack(col_filters, col_block, col_block + 2 * RAD)
    masked = masked_planes(variance, mask_bits, boxes, col_first)
    extended = extended_2(image, (("sky", 2),), RAD)
    padded = jnp.pad(extended, ((0, 0), (RAD, RAD), (0, 0)))
    windows = column_windows(padded, col_block, RAD)
    weights = inverse_weight(masked)
    slab_windows = windows[0]
    matched = match_rows(
        slab_windows,
        coeffs[0],
        lax.axis_size("visit") * ROWS_DEV,
        col_first,
        height,
        width,
        row_mats,
        col_mats,
    )
    weight_rows = weights[0]
    numer_part = weight_rows * matched
    numerator, denominator = lax.psum_scatter(
        (numer_part, weight_rows), "visit", scatter_dimension=0, tiled=True
    )
    coadd = numerator / jnp.maximum(denominator, 1.0)
    return (coadd, denominator)


def solution(mesh):
    in_specs = (
        P("visit", None, "sky"),
        P("visit", None, "sky"),
        P("visit", None, "sky"),
        P("visit", None),
        P(),
        P(),
        P("visit", None, None),
    )
    out_specs = (P("visit", "sky"), P("visit", "sky"))
    return jax.shard_map(
        per_device, mesh=mesh, in_specs=in_specs, out_specs=out_specs, check_vma=False
    )
```

profile of v0, /device:TPU:0, one launch (start us, length us, event | category | flops | bytes accessed | tf_op | source)
XLA Modules:
  0.0 284.7 jit_solution(6205631911827444698)
XLA Ops:
  8.5 4.9 %collective-permute-start = (bf16[1,384,20]{1,2,0:T(8,128)(2,1)S(1)}, bf16[1,384,20]{1,2,0:T(8,128)(2,1)S(1)}, u32[]{:S(2)}, u32[]{:S(2)}) collective-permute-start(bf16[1,384,20]{1,2,0:T(8,128)(2,1)S(1)} %get-tuple-element.249), channel_id=1, source_target_pairs={{0,1},{1,2},{2,3},{4,5},{5,6},{6,7},{8,9},{9,10},{10,11},{12,13},{... | collective-permute-start | bytes 46088 | tf_op jit(solution)/shard_map/ppermute | solution.py:20
  23.8 173.6 %while.15 = (s32[]{:T(128)}, f32[8,48,4,128]{3,1,2,0:T(8,128)}, f32[20,6]{0,1:T(8,128)S(1)}, bf16[20,128,168]{2,1,0:T(8,128)(2,1)S(1)}, bf16[424,4,168]{2,1,0:T(...) while((s32[]{:T(128)}, f32[8,48,4,128]{3,1,2,0:T(8,128)}, ...), condition=%wide.region_1.2_spmd.clone.clone.clone.clone, body=%wide.region_0.1_spmd.clone.clone.clone.clone.sunk | while | flops 109547952 | bytes 6007147 | solution.py:104
  29.5 2.6 fusion.68
  37.7 3.0 %fusion.68 = f32[8,48,4,128]{3,1,2,0:T(8,128)} fusion(f32[8,48,4,128]{3,1,2,0:T(8,128)} %get-tuple-element.330, bf16[8,88,4,128]{3,2,1,0:T(4,128)(2,1)S(1)} %gather_fusion, f32[8,48]{1,0:T(8,128)S(1)} %get-tuple-element.311, f32[8,48]{1,0:T(8,128)S(1)} %get-tuple-element.312, f32[4,128]{1,0:T(4,128)S(1)} %get-tuple-element.314, f32[]{:T(128)} %bitcast.104, ...), kind=kOutput, calls=%fused_computation.8.clone.1 | convolution fusion | flops 36372480 | bytes 2317825 | tf_op jit(solution)/shard_map/while/body/eval_jaxpr/sr,nrkc->nskc/dot_general | solution.py:100
  46.4 3.0 %fusion.68 = f32[8,48,4,128]{3,1,2,0:T(8,128)} fusion(f32[8,48,4,128]{3,1,2,0:T(8,128)} %get-tuple-element.330, bf16[8,88,4,128]{3,2,1,0:T(4,128)(2,1)S(1)} %gather_fusion, f32[8,48]{1,0:T(8,128)S(1)} %get-tuple-element.311, f32[8,48]{1,0:T(8,128)S(1)} %get-tuple-element.312, f32[4,128]{1,0:T(4,128)S(1)} %get-tuple-element.314, f32[]{:T(128)} %bitcast.104, ...), kind=kOutput, calls=%fused_computation.8.clone.1 | convolution fusion | flops 36372480 | bytes 2317825 | tf_op jit(solution)/shard_map/while/body/eval_jaxpr/sr,nrkc->nskc/dot_general | solution.py:100
  55.1 3.0 %fusion.68 = f32[8,48,4,128]{3,1,2,0:T(8,128)} fusion(f32[8,48,4,128]{3,1,2,0:T(8,128)} %get-tuple-element.330, bf16[8,88,4,128]{3,2,1,0:T(4,128)(2,1)S(1)} %gather_fusion, f32[8,48]{1,0:T(8,128)S(1)} %get-tuple-element.311, f32[8,48]{1,0:T(8,128)S(1)} %get-tuple-element.312, f32[4,128]{1,0:T(4,128)S(1)} %get-tuple-element.314, f32[]{:T(128)} %bitcast.104, ...), kind=kOutput, calls=%fused_computation.8.clone.1 | convolution fusion | flops 36372480 | bytes 2317825 | tf_op jit(solution)/shard_map/while/body/eval_jaxpr/sr,nrkc->nskc/dot_general | solution.py:100
  63.8 3.0 %fusion.68 = f32[8,48,4,128]{3,1,2,0:T(8,128)} fusion(f32[8,48,4,128]{3,1,2,0:T(8,128)} %get-tuple-element.330, bf16[8,88,4,128]{3,2,1,0:T(4,128)(2,1)S(1)} %gather_fusion, f32[8,48]{1,0:T(8,128)S(1)} %get-tuple-element.311, f32[8,48]{1,0:T(8,128)S(1)} %get-tuple-element.312, f32[4,128]{1,0:T(4,128)S(1)} %get-tuple-element.314, f32[]{:T(128)} %bitcast.104, ...), kind=kOutput, calls=%fused_computation.8.clone.1 | convolution fusion | flops 36372480 | bytes 2317825 | tf_op jit(solution)/shard_map/while/body/eval_jaxpr/sr,nrkc->nskc/dot_general | solution.py:100
  72.5 3.0 %fusion.68 = f32[8,48,4,128]{3,1,2,0:T(8,128)} fusion(f32[8,48,4,128]{3,1,2,0:T(8,128)} %get-tuple-element.330, bf16[8,88,4,128]{3,2,1,0:T(4,128)(2,1)S(1)} %gather_fusion, f32[8,48]{1,0:T(8,128)S(1)} %get-tuple-element.311, f32[8,48]{1,0:T(8,128)S(1)} %get-tuple-element.312, f32[4,128]{1,0:T(4,128)S(1)} %get-tuple-element.314, f32[]{:T(128)} %bitcast.104, ...), kind=kOutput, calls=%fused_computation.8.clone.1 | convolution fusion | flops 36372480 | bytes 2317825 | tf_op jit(solution)/shard_map/while/body/eval_jaxpr/sr,nrkc->nskc/dot_general | solution.py:100
  81.2 3.0 %fusion.68 = f32[8,48,4,128]{3,1,2,0:T(8,128)} fusion(f32[8,48,4,128]{3,1,2,0:T(8,128)} %get-tuple-element.330, bf16[8,88,4,128]{3,2,1,0:T(4,128)(2,1)S(1)} %gather_fusion, f32[8,48]{1,0:T(8,128)S(1)} %get-tuple-element.311, f32[8,48]{1,0:T(8,128)S(1)} %get-tuple-element.312, f32[4,128]{1,0:T(4,128)S(1)} %get-tuple-element.314, f32[]{:T(128)} %bitcast.104, ...), kind=kOutput, calls=%fused_computation.8.clone.1 | convolution fusion | flops 36372480 | bytes 2317825 | tf_op jit(solution)/shard_map/while/body/eval_jaxpr/sr,nrkc->nskc/dot_general | solution.py:100
  89.9 3.0 %fusion.68 = f32[8,48,4,128]{3,1,2,0:T(8,128)} fusion(f32[8,48,4,128]{3,1,2,0:T(8,128)} %get-tuple-element.330, bf16[8,88,4,128]{3,2,1,0:T(4,128)(2,1)S(1)} %gather_fusion, f32[8,48]{1,0:T(8,128)S(1)} %get-tuple-element.311, f32[8,48]{1,0:T(8,128)S(1)} %get-tuple-element.312, f32[4,128]{1,0:T(4,128)S(1)} %get-tuple-element.314, f32[]{:T(128)} %bitcast.104, ...), kind=kOutput, calls=%fused_computation.8.clone.1 | convolution fusion | flops 36372480 | bytes 2317825 | tf_op jit(solution)/shard_map/while/body/eval_jaxpr/sr,nrkc->nskc/dot_general | solution.py:100
  98.6 3.0 %fusion.68 = f32[8,48,4,128]{3,1,2,0:T(8,128)} fusion(f32[8,48,4,128]{3,1,2,0:T(8,128)} %get-tuple-element.330, bf16[8,88,4,128]{3,2,1,0:T(4,128)(2,1)S(1)} %gather_fusion, f32[8,48]{1,0:T(8,128)S(1)} %get-tuple-element.311, f32[8,48]{1,0:T(8,128)S(1)} %get-tuple-element.312, f32[4,128]{1,0:T(4,128)S(1)} %get-tuple-element.314, f32[]{:T(128)} %bitcast.104, ...), kind=kOutput, calls=%fused_computation.8.clone.1 | convolution fusion | flops 36372480 | bytes 2317825 | tf_op jit(solution)/shard_map/while/body/eval_jaxpr/sr,nrkc->nskc/dot_general | solution.py:100
  107.3 3.0 %fusion.68 = f32[8,48,4,128]{3,1,2,0:T(8,128)} fusion(f32[8,48,4,128]{3,1,2,0:T(8,128)} %get-tuple-element.330, bf16[8,88,4,128]{3,2,1,0:T(4,128)(2,1)S(1)} %gather_fusion, f32[8,48]{1,0:T(8,128)S(1)} %get-tuple-element.311, f32[8,48]{1,0:T(8,128)S(1)} %get-tuple-element.312, f32[4,128]{1,0:T(4,128)S(1)} %get-tuple-element.314, f32[]{:T(128)} %bitcast.104, ...), kind=kOutput, calls=%fused_computation.8.clone.1 | convolution fusion | flops 36372480 | bytes 2317825 | tf_op jit(solution)/shard_map/while/body/eval_jaxpr/sr,nrkc->nskc/dot_general | solution.py:100
  116.1 3.0 %fusion.68 = f32[8,48,4,128]{3,1,2,0:T(8,128)} fusion(f32[8,48,4,128]{3,1,2,0:T(8,128)} %get-tuple-element.330, bf16[8,88,4,128]{3,2,1,0:T(4,128)(2,1)S(1)} %gather_fusion, f32[8,48]{1,0:T(8,128)S(1)} %get-tuple-element.311, f32[8,48]{1,0:T(8,128)S(1)} %get-tuple-element.312, f32[4,128]{1,0:T(4,128)S(1)} %get-tuple-element.314, f32[]{:T(128)} %bitcast.104, ...), kind=kOutput, calls=%fused_computation.8.clone.1 | convolution fusion | flops 36372480 | bytes 2317825 | tf_op jit(solution)/shard_map/while/body/eval_jaxpr/sr,nrkc->nskc/dot_general | solution.py:100
  124.8 3.0 %fusion.68 = f32[8,48,4,128]{3,1,2,0:T(8,128)} fusion(f32[8,48,4,128]{3,1,2,0:T(8,128)} %get-tuple-element.330, bf16[8,88,4,128]{3,2,1,0:T(4,128)(2,1)S(1)} %gather_fusion, f32[8,48]{1,0:T(8,128)S(1)} %get-tuple-element.311, f32[8,48]{1,0:T(8,128)S(1)} %get-tuple-element.312, f32[4,128]{1,0:T(4,128)S(1)} %get-tuple-element.314, f32[]{:T(128)} %bitcast.104, ...), kind=kOutput, calls=%fused_computation.8.clone.1 | convolution fusion | flops 36372480 | bytes 2317825 | tf_op jit(solution)/shard_map/while/body/eval_jaxpr/sr,nrkc->nskc/dot_general | solution.py:100
  133.5 3.0 %fusion.68 = f32[8,48,4,128]{3,1,2,0:T(8,128)} fusion(f32[8,48,4,128]{3,1,2,0:T(8,128)} %get-tuple-element.330, bf16[8,88,4,128]{3,2,1,0:T(4,128)(2,1)S(1)} %gather_fusion, f32[8,48]{1,0:T(8,128)S(1)} %get-tuple-element.311, f32[8,48]{1,0:T(8,128)S(1)} %get-tuple-element.312, f32[4,128]{1,0:T(4,128)S(1)} %get-tuple-element.314, f32[]{:T(128)} %bitcast.104, ...), kind=kOutput, calls=%fused_computation.8.clone.1 | convolution fusion | flops 36372480 | bytes 2317825 | tf_op jit(solution)/shard_map/while/body/eval_jaxpr/sr,nrkc->nskc/dot_general | solution.py:100
  142.2 3.0 %fusion.68 = f32[8,48,4,128]{3,1,2,0:T(8,128)} fusion(f32[8,48,4,128]{3,1,2,0:T(8,128)} %get-tuple-element.330, bf16[8,88,4,128]{3,2,1,0:T(4,128)(2,1)S(1)} %gather_fusion, f32[8,48]{1,0:T(8,128)S(1)} %get-tuple-element.311, f32[8,48]{1,0:T(8,128)S(1)} %get-tuple-element.312, f32[4,128]{1,0:T(4,128)S(1)} %get-tuple-element.314, f32[]{:T(128)} %bitcast.104, ...), kind=kOutput, calls=%fused_computation.8.clone.1 | convolution fusion | flops 36372480 | bytes 2317825 | tf_op jit(solution)/shard_map/while/body/eval_jaxpr/sr,nrkc->nskc/dot_general | solution.py:100
  150.9 3.0 %fusion.68 = f32[8,48,4,128]{3,1,2,0:T(8,128)} fusion(f32[8,48,4,128]{3,1,2,0:T(8,128)} %get-tuple-element.330, bf16[8,88,4,128]{3,2,1,0:T(4,128)(2,1)S(1)} %gather_fusion, f32[8,48]{1,0:T(8,128)S(1)} %get-tuple-element.311, f32[8,48]{1,0:T(8,128)S(1)} %get-tuple-element.312, f32[4,128]{1,0:T(4,128)S(1)} %get-tuple-element.314, f32[]{:T(128)} %bitcast.104, ...), kind=kOutput, calls=%fused_computation.8.clone.1 | convolution fusion | flops 36372480 | bytes 2317825 | tf_op jit(solution)/shard_map/while/body/eval_jaxpr/sr,nrkc->nskc/dot_general | solution.py:100
  159.6 3.0 %fusion.68 = f32[8,48,4,128]{3,1,2,0:T(8,128)} fusion(f32[8,48,4,128]{3,1,2,0:T(8,128)} %get-tuple-element.330, bf16[8,88,4,128]{3,2,1,0:T(4,128)(2,1)S(1)} %gather_fusion, f32[8,48]{1,0:T(8,128)S(1)} %get-tuple-element.311, f32[8,48]{1,0:T(8,128)S(1)} %get-tuple-element.312, f32[4,128]{1,0:T(4,128)S(1)} %get-tuple-element.314, f32[]{:T(128)} %bitcast.104, ...), kind=kOutput, calls=%fused_computation.8.clone.1 | convolution fusion | flops 36372480 | bytes 2317825 | tf_op jit(solution)/shard_map/while/body/eval_jaxpr/sr,nrkc->nskc/dot_general | solution.py:100
  168.3 3.0 %fusion.68 = f32[8,48,4,128]{3,1,2,0:T(8,128)} fusion(f32[8,48,4,128]{3,1,2,0:T(8,128)} %get-tuple-element.330, bf16[8,88,4,128]{3,2,1,0:T(4,128)(2,1)S(1)} %gather_fusion, f32[8,48]{1,0:T(8,128)S(1)} %get-tuple-element.311, f32[8,48]{1,0:T(8,128)S(1)} %get-tuple-element.312, f32[4,128]{1,0:T(4,128)S(1)} %get-tuple-element.314, f32[]{:T(128)} %bitcast.104, ...), kind=kOutput, calls=%fused_computation.8.clone.1 | convolution fusion | flops 36372480 | bytes 2317825 | tf_op jit(solution)/shard_map/while/body/eval_jaxpr/sr,nrkc->nskc/dot_general | solution.py:100
  177.0 3.0 %fusion.68 = f32[8,48,4,128]{3,1,2,0:T(8,128)} fusion(f32[8,48,4,128]{3,1,2,0:T(8,128)} %get-tuple-element.330, bf16[8,88,4,128]{3,2,1,0:T(4,128)(2,1)S(1)} %gather_fusion, f32[8,48]{1,0:T(8,128)S(1)} %get-tuple-element.311, f32[8,48]{1,0:T(8,128)S(1)} %get-tuple-element.312, f32[4,128]{1,0:T(4,128)S(1)} %get-tuple-element.314, f32[]{:T(128)} %bitcast.104, ...), kind=kOutput, calls=%fused_computation.8.clone.1 | convolution fusion | flops 36372480 | bytes 2317825 | tf_op jit(solution)/shard_map/while/body/eval_jaxpr/sr,nrkc->nskc/dot_general | solution.py:100
  185.7 3.0 %fusion.68 = f32[8,48,4,128]{3,1,2,0:T(8,128)} fusion(f32[8,48,4,128]{3,1,2,0:T(8,128)} %get-tuple-element.330, bf16[8,88,4,128]{3,2,1,0:T(4,128)(2,1)S(1)} %gather_fusion, f32[8,48]{1,0:T(8,128)S(1)} %get-tuple-element.311, f32[8,48]{1,0:T(8,128)S(1)} %get-tuple-element.312, f32[4,128]{1,0:T(4,128)S(1)} %get-tuple-element.314, f32[]{:T(128)} %bitcast.104, ...), kind=kOutput, calls=%fused_computation.8.clone.1 | convolution fusion | flops 36372480 | bytes 2317825 | tf_op jit(solution)/shard_map/while/body/eval_jaxpr/sr,nrkc->nskc/dot_general | solution.py:100
  194.4 3.0 %fusion.68 = f32[8,48,4,128]{3,1,2,0:T(8,128)} fusion(f32[8,48,4,128]{3,1,2,0:T(8,128)} %get-tuple-element.330, bf16[8,88,4,128]{3,2,1,0:T(4,128)(2,1)S(1)} %gather_fusion, f32[8,48]{1,0:T(8,128)S(1)} %get-tuple-element.311, f32[8,48]{1,0:T(8,128)S(1)} %get-tuple-element.312, f32[4,128]{1,0:T(4,128)S(1)} %get-tuple-element.314, f32[]{:T(128)} %bitcast.104, ...), kind=kOutput, calls=%fused_computation.8.clone.1 | convolution fusion | flops 36372480 | bytes 2317825 | tf_op jit(solution)/shard_map/while/body/eval_jaxpr/sr,nrkc->nskc/dot_general | solution.py:100
  201.3 36.7 %reduce-scatter.5.cloned.1.call-done = f32[48,512]{1,0:T(8,128)} async-done(((f32[384,512]{1,0:T(8,128)}), f32[48,512]{1,0:T(8,128)}) %reduce-scatter.5.cloned.1.call-update) | async-done | bytes 98320 | tf_op jit(solution)/shard_map/reduce_scatter | solution.py:134
  238.1 38.2 %reduce-scatter.3.cloned.1.call-done = f32[48,512]{1,0:T(8,128)} async-done(((f32[384,512]{1,0:T(8,128)}), f32[48,512]{1,0:T(8,128)}) %reduce-scatter.3.cloned.1.call-update) | async-done | bytes 98320 | tf_op jit(solution)/shard_map/reduce_scatter | solution.py:134
  (237 shorter events, 129.2 us)
Async XLA Ops:
  7.2 9.0 %copy-start = (bf16[20,41]{1,0:T(8,128)(2,1)S(1)}, bf16[20,41]{1,0:T(8,128)(2,1)}, u32[]{:S(2)}) copy-start(bf16[20,41]{1,0:T(8,128)(2,1)} %param.14) | copy-start | bytes 4924
  7.2 10.0 %copy-start.4 = (bf16[20,41]{1,0:T(8,128)(2,1)S(1)}, bf16[20,41]{1,0:T(8,128)(2,1)}, u32[]{:S(2)}) copy-start(bf16[20,41]{1,0:T(8,128)(2,1)} %param.13) | copy-start | bytes 4924
  7.2 230.9 %reduce-scatter.5.cloned.1.call-start = ((), (), s32[]{:S(2)}) async-start(), calls=%async_computation.3 | async-start | bytes 884736 | tf_op jit(solution)/shard_map/reduce_scatter | solution.py:134
  8.5 13.8 %collective-permute-start = (bf16[1,384,20]{1,2,0:T(8,128)(2,1)S(1)}, bf16[1,384,20]{1,2,0:T(8,128)(2,1)S(1)}, u32[]{:S(2)}, u32[]{:S(2)}) collective-permute-start(bf16[1,384,20]{1,2,0:T(8,128)(2,1)S(1)} %get-tuple-element.249), channel_id=1, source_target_pairs={{0,1},{1,2},{2,3},{4,5},{5,6},{6,7},{8,9},{9,10},{10,11},{12,13},{... | collective-permute-start | bytes 46088 | tf_op jit(solution)/shard_map/ppermute | solution.py:20
  13.4 8.8 %collective-permute-start.1 = (bf16[1,384,20]{1,2,0:T(8,128)(2,1)S(1)}, bf16[1,384,20]{1,2,0:T(8,128)(2,1)S(1)}, u32[]{:S(2)}, u32[]{:S(2)}) collective-permute-start(bf16[1,384,20]{1,2,0:T(8,128)(2,1)S(1)} %get-tuple-element.250), channel_id=1, source_target_pairs={{1,0},{2,1},{3,2},{5,4},{6,5},{7,6},{9,8},{10,9},{11,10},{13,12},{... | collective-permute-start | bytes 46088 | tf_op jit(solution)/shard_map/ppermute | solution.py:21
  20.0 2.2 copy-start.3
  197.4 1.5 copy-start.1
  197.4 1.6 copy-start.2
  200.6 75.6 %reduce-scatter.3.cloned.1.call-start = ((), (), s32[]{:S(2)}) async-start(), calls=%async_computation.2 | async-start | bytes 884736 | tf_op jit(solution)/shard_map/reduce_scatter | solution.py:134
Sparse Core Ops, SparseCore 0:
  200.7 37.3 reduce-scatter.4
  241.2 34.9 reduce-scatter.2
where the time goes:
time: 287 us; the launch traced here: 285 us
  waiting for transfers between devices  75.6 us (26%)
  other arithmetic  70.1 us (24%)
  matrix products  69.9 us (24%)
  local copies, waits for them, and re-layouts  47.7 us (17%)
  between operations  14.2 us (5%)
  starting transfers between devices  6.3 us (2%)
    reduce_scatter x2, waiting for transfers between devices, per_device(): lax.psum_scatter((numer_part, weight_rows), 'visit', scatter_dimension=0,...  74.9 us
    dot_general x20, matrix products, basis_step(): jnp.einsum('sr,nrkc->nskc', row_mat, bands, preferred_element_type=jnp.fl...  60.5 us
    add x20, other arithmetic, poly_field(): factors[0] + factors[1] * xcoord + factors[2] * ycoord  25.4 us
    gather x20, local copies, waits for them, and re-layouts, basis_step(): lax.dynamic_slice_in_dim(colpass, first_row, window_rows, 0)  23.3 us
    mul x20, other arithmetic, poly_field(): factors[5] * (ycoord * ycoord)  13.7 us
    mul x20, other arithmetic, poly_field(): factors[2] * ycoord  12.9 us
    slice x20, local copies, waits for them, and re-layouts, poly_field(): factors[0] + factors[1] * xcoord + factors[2] * ycoord  12.1 us
    mul x20, other arithmetic, poly_field(): factors[3] * (xcoord * xcoord)  11.7 us
  transfers between devices with their start and end apart: 4, of which 2 were waited for; matrix products, arithmetic and copies ran while one was open for 3% of the time, Pallas kernels for 0%

commit v1 on v0

v1 whole, which is shorter than its diff:
```python
import functools

import jax
import jax.numpy as jnp
from jax import lax
from jax.experimental import pallas as pl
from jax.experimental.pallas import tpu as pltpu
from jax.sharding import PartitionSpec as P

RAD = 20
ROWS_DEV = 48
REJECT = 7
LANES = 128
GROUP = 4
BAND = GROUP * ROWS_DEV
PAD = 32
WIN = BAND + 2 * PAD
MESH = pl.DeviceIdType.MESH


def kernel(
    visits,
    skies,
    image_ref,
    var_ref,
    bits_ref,
    boxes_ref,
    rowf_ref,
    colf_ref,
    coef_ref,
    coadd_ref,
    wsum_ref,
    halo_l,
    halo_r,
    masked,
    got_var,
    matched,
    got_pix,
    total,
    windows,
    row_mats,
    col_mats,
    colpass,
    filt,
    var_send,
    var_recv,
    pix_send,
    pix_recv,
    halo_send,
    halo_recv,
):
    height, cols = image_ref.shape[1], image_ref.shape[2]
    width = cols * skies
    basis, taps = rowf_ref.shape
    blocks = cols // LANES
    groups = visits // GROUP
    v = lax.axis_index("visit")
    z = lax.axis_index("sky")
    my_group = v // GROUP
    has_l = z > 0
    has_r = z < skies - 1

    barrier = pltpu.get_barrier_semaphore()
    for step in range(1, visits):
        pl.semaphore_signal(
            barrier, inc=1, device_id=(lax.rem(v + step, visits), z), device_id_type=MESH
        )

    @pl.when(has_l)
    def _():
        pl.semaphore_signal(barrier, inc=1, device_id=(v, z - 1), device_id_type=MESH)

    @pl.when(has_r)
    def _():
        pl.semaphore_signal(barrier, inc=1, device_id=(v, z + 1), device_id_type=MESH)

    col_first = z * cols
    box = [boxes_ref[0, i] for i in range(4)]
    col_index = col_first + lax.broadcasted_iota(jnp.int32, (ROWS_DEV, cols), 1)
    col_inside = (col_index >= box[2]) & (col_index < box[3])
    row_iota = lax.broadcasted_iota(jnp.int32, (ROWS_DEV, cols), 0)

    def mask_band(band, carry):
        first = pl.multiple_of(band * ROWS_DEV, ROWS_DEV)
        rows = pl.ds(first, ROWS_DEV)
        row_index = first + row_iota
        inside = (row_index >= box[0]) & (row_index < box[1]) & col_inside
        inside = inside & ((bits_ref[0, rows, :] & REJECT) == 0)
        masked[rows, :] = jnp.where(inside, var_ref[0, rows, :].astype(jnp.float32), 0.0).astype(
            jnp.bfloat16
        )
        return carry

    lax.fori_loop(0, visits, mask_band, 0)

    pl.semaphore_wait(barrier, visits - 1 + has_l.astype(jnp.int32) + has_r.astype(jnp.int32))

    send_left = pltpu.make_async_remote_copy(
        src_ref=image_ref.at[0, :, pl.ds(0, LANES)],
        dst_ref=halo_r,
        send_sem=halo_send.at[0],
        recv_sem=halo_recv.at[1],
        device_id=(v, z - 1),
        device_id_type=MESH,
    )
    send_right = pltpu.make_async_remote_copy(
        src_ref=image_ref.at[0, :, pl.ds(cols - LANES, LANES)],
        dst_ref=halo_l,
        send_sem=halo_send.at[1],
        recv_sem=halo_recv.at[0],
        device_id=(v, z + 1),
        device_id_type=MESH,
    )

    @pl.when(has_l)
    def _():
        send_left.start()

    @pl.when(has_r)
    def _():
        send_right.start()

    def band_copy(src, dst, send, recv, dest):
        return pltpu.make_async_remote_copy(
            src_ref=src.at[pl.ds(pl.multiple_of(dest * ROWS_DEV, ROWS_DEV), ROWS_DEV), :],
            dst_ref=dst.at[v],
            send_sem=send.at[dest],
            recv_sem=recv.at[v],
            device_id=(dest, z),
            device_id_type=MESH,
        )

    def var_copy(dest):
        return band_copy(masked, got_var, var_send, var_recv, dest)

    def pix_copy(dest):
        return band_copy(matched, got_pix, pix_send, pix_recv, dest)

    for step in range(1, visits):
        var_copy(lax.rem(v + step, visits)).start()

    filt[...] = jnp.zeros_like(filt)
    filt[0, 0:basis, 0:taps] = rowf_ref[...].astype(jnp.float32)
    filt[1, 0:basis, 0:taps] = colf_ref[...].astype(jnp.float32)
    filt[0] = pltpu.roll(filt[0], PAD - RAD, 1)

    def build(b, carry):
        row = jnp.broadcast_to(filt[0, pl.ds(b, 1), :], (BAND, WIN))
        row_mats[b] = pltpu.roll(row, 0, 1, stride=1, stride_axis=0).astype(jnp.bfloat16)
        col = jnp.broadcast_to(filt[1, pl.ds(b, 1), :], (LANES, 2 * LANES))
        col_mats[b] = pltpu.roll(col, 0, 1, stride=1, stride_axis=0).astype(jnp.bfloat16)
        return carry

    lax.fori_loop(0, basis, build, 0)

    @pl.when(has_l)
    def _():
        send_right_here = pltpu.make_async_remote_copy(
            src_ref=image_ref.at[0, :, pl.ds(0, LANES)],
            dst_ref=halo_l,
            send_sem=halo_send.at[0],
            recv_sem=halo_recv.at[0],
            device_id=(v, z - 1),
            device_id_type=MESH,
        )
        send_right_here.wait_recv()

    @pl.when(jnp.logical_not(has_l))
    def _():
        halo_l[...] = jnp.zeros_like(halo_l)

    @pl.when(has_r)
    def _():
        pltpu.make_async_remote_copy(
            src_ref=image_ref.at[0, :, pl.ds(0, LANES)],
            dst_ref=halo_r,
            send_sem=halo_send.at[1],
            recv_sem=halo_recv.at[1],
            device_id=(v, z + 1),
            device_id_type=MESH,
        ).wait_recv()

    @pl.when(jnp.logical_not(has_r))
    def _():
        halo_r[...] = jnp.zeros_like(halo_r)

    for k in range(blocks):
        windows[k, 0:PAD, :] = jnp.zeros((PAD, 2 * LANES), jnp.bfloat16)
        windows[k, PAD + height : PAD + height + PAD, :] = jnp.zeros((PAD, 2 * LANES), jnp.bfloat16)

    def shift_band(band, carry):
        first = pl.multiple_of(band * ROWS_DEV, ROWS_DEV)
        rows = pl.ds(first, ROWS_DEV)
        wide = jnp.concatenate(
            [halo_l[rows, :], image_ref[0, rows, :], halo_r[rows, :]], axis=1
        ).astype(jnp.float32)
        total_lanes = cols + 2 * LANES
        wide = pltpu.roll(wide, total_lanes - (LANES - RAD), 1).astype(jnp.bfloat16)
        dest = pl.ds(pl.multiple_of(first + PAD, 16), ROWS_DEV)
        for k in range(blocks):
            windows[k, dest, :] = wide[:, k * LANES : (k + 2) * LANES]
        return carry

    lax.fori_loop(0, visits, shift_band, 0)

    col_pos = (col_first + lax.broadcasted_iota(jnp.int32, (1, cols), 1)).astype(jnp.float32)
    xc = (2.0 * col_pos + 1.0) / width - 1.0
    xx = xc * xc
    y_iota = lax.broadcasted_iota(jnp.int32, (BAND, LANES), 0)

    def one_group(step, carry):
        group = lax.rem(my_group + 1 + step, groups)
        first = pl.multiple_of(group * BAND, BAND)
        yc = (2.0 * (first + y_iota).astype(jnp.float32) + 1.0) / height - 1.0
        total[...] = jnp.zeros_like(total)

        def pair_step(p, inner):
            image_win = windows[:, pl.ds(first, WIN), :].reshape(blocks * WIN, 2 * LANES)
            mats = col_mats[pl.ds(2 * p, 2)].reshape(2 * LANES, 2 * LANES)
            passed = lax.dot_general(
                image_win, mats, (((1,), (1,)), ((), ())), preferred_element_type=jnp.float32
            ).astype(jnp.bfloat16)
            for k in range(blocks):
                for h in range(2):
                    colpass[h, :, k * LANES : (k + 1) * LANES] = passed[
                        k * WIN : (k + 1) * WIN, h * LANES : (h + 1) * LANES
                    ]
            parts = []
            for h in range(2):
                b = 2 * p + h
                c = [coef_ref[0, b, t] for t in range(6)]
                rowpass = jnp.dot(row_mats[b], colpass[h], preferred_element_type=jnp.float32)
                in_x = c[0] + c[1] * xc + c[3] * xx
                in_xy = c[2] + c[4] * xc
                in_yy = c[5] * yc
                parts.append((rowpass, in_x, in_xy, in_yy))
            for k in range(blocks):
                lanes = slice(k * LANES, (k + 1) * LANES)
                add = total[:, lanes]
                for rowpass, in_x, in_xy, in_yy in parts:
                    field = in_x[:, lanes] + yc * (in_xy[:, lanes] + in_yy)
                    add = add + field * rowpass[:, lanes]
                total[:, lanes] = add
            return inner

        lax.fori_loop(0, basis // 2, pair_step, 0)
        matched[pl.ds(first, BAND), :] = total[...].astype(jnp.bfloat16)
        for j in range(GROUP):
            dest = group * GROUP + j

            @pl.when(dest != v)
            def _():
                pix_copy(dest).start()

        return carry

    lax.fori_loop(0, groups, one_group, 0)

    own_rows = pl.ds(pl.multiple_of(v * ROWS_DEV, ROWS_DEV), ROWS_DEV)

    def weight_of(plane):
        plane = plane.astype(jnp.float32)
        positive = plane > 0
        return jnp.where(positive, 1.0 / jnp.where(positive, plane, 1.0), 0.0)

    own_first = pl.multiple_of((v - my_group * GROUP) * ROWS_DEV, ROWS_DEV)
    own_weight = weight_of(masked[own_rows, :])
    coadd_ref[...] = own_weight * total[pl.ds(own_first, ROWS_DEV), :]
    wsum_ref[...] = own_weight

    def recv_wait(dst, send, recv, source):
        pltpu.make_async_remote_copy(
            src_ref=masked.at[pl.ds(0, ROWS_DEV), :],
            dst_ref=dst.at[source],
            send_sem=send.at[source],
            recv_sem=recv.at[source],
            device_id=(source, z),
            device_id_type=MESH,
        ).wait_recv()

    def add_source(step, carry):
        source = lax.rem(v + step, visits)
        recv_wait(got_var, var_send, var_recv, source)
        weight = weight_of(got_var[source])
        wsum_ref[...] += weight
        recv_wait(got_pix, pix_send, pix_recv, source)
        coadd_ref[...] += weight * got_pix[source].astype(jnp.float32)
        return carry

    lax.fori_loop(1, visits, add_source, 0)
    coadd_ref[...] = coadd_ref[...] / jnp.maximum(wsum_ref[...], 1.0)

    for step in range(1, visits):
        dest = lax.rem(v + step, visits)
        var_copy(dest).wait_send()
        pix_copy(dest).wait_send()

    @pl.when(has_l)
    def _():
        send_left.wait_send()

    @pl.when(has_r)
    def _():
        send_right.wait_send()


def per_device(image, variance, mask_bits, boxes, row_filters, col_filters, coeffs):
    height, cols = image.shape[1], image.shape[2]
    visits, skies = lax.axis_size("visit"), lax.axis_size("sky")
    basis = row_filters.shape[0]
    blocks = cols // LANES
    vmem = pl.BlockSpec(memory_space=pltpu.VMEM)
    smem = pl.BlockSpec(memory_space=pltpu.SMEM)
    band = jax.ShapeDtypeStruct((ROWS_DEV, cols), jnp.float32)
    bf16 = jnp.bfloat16
    dma = pltpu.SemaphoreType.DMA
    return pl.pallas_call(
        functools.partial(kernel, visits, skies),
        out_shape=(band, band),
        in_specs=[vmem, vmem, vmem, smem, vmem, vmem, smem],
        out_specs=(vmem, vmem),
        scratch_shapes=[
            pltpu.VMEM((height, LANES), bf16),
            pltpu.VMEM((height, LANES), bf16),
            pltpu.VMEM((height, cols), bf16),
            pltpu.VMEM((visits, ROWS_DEV, cols), bf16),
            pltpu.VMEM((height, cols), bf16),
            pltpu.VMEM((visits, ROWS_DEV, cols), bf16),
            pltpu.VMEM((BAND, cols), jnp.float32),
            pltpu.VMEM((blocks, height + 2 * PAD, 2 * LANES), bf16),
            pltpu.VMEM((basis, BAND, WIN), bf16),
            pltpu.VMEM((basis, LANES, 2 * LANES), bf16),
            pltpu.VMEM((2, WIN, cols), bf16),
            pltpu.VMEM((2, 24, WIN), jnp.float32),
            dma((visits,)),
            dma((visits,)),
            dma((visits,)),
            dma((visits,)),
            dma((2,)),
            dma((2,)),
        ],
        compiler_params=pltpu.CompilerParams(
            collective_id=0, has_side_effects=True, vmem_limit_bytes=40 * 1024 * 1024
        ),
    )(image, variance, mask_bits, boxes, row_filters, col_filters, coeffs)


def solution(mesh):
    in_specs = (
        P("visit", None, "sky"),
        P("visit", None, "sky"),
        P("visit", None, "sky"),
        P("visit", None),
        P(),
        P(),
        P("visit", None, None),
    )
    out_specs = (P("visit", "sky"), P("visit", "sky"))
    return jax.shard_map(
        per_device, mesh=mesh, in_specs=in_specs, out_specs=out_specs, check_vma=False
    )
```

time: 287 us -> 35.3 us (0.12)
  waiting for transfers between devices: 75.6 us -> 0 us
  other arithmetic: 70.1 us -> 0 us
  matrix products: 69.9 us -> 0 us
  local copies, waits for them, and re-layouts: 47.7 us -> 5.21 us
  Pallas kernels: 0 us -> 29.2 us
  between operations: 14.2 us -> 0.68 us
  starting transfers between devices: 6.3 us -> 0 us
    reduce_scatter x2 -> x0, waiting for transfers between devices: 74.9 us -> none  [per_device(): lax.psum_scatter((numer_part, weight_rows), 'visit', scatter_dimension=0,...]
    dot_general x42 -> x0, matrix products: 69.9 us -> none  [the longest x20 60.5 us: basis_step(): jnp.einsum('sr,nrkc->nskc', row_mat, bands, preferred_element_type=jnp.fl...]
    mul x61 -> x0, other arithmetic: 39.9 us -> none  [the longest x20 13.7 us: poly_field(): factors[5] * (ycoord * ycoord)]
    pallas_call x0 -> x1, Pallas kernels: none -> 29.2 us  [per_device(): pl.pallas_call(functools.partial(kernel, visits, skies), out_shape=(band,...]
    add x20 -> x0, other arithmetic: 25.4 us -> none  [poly_field(): factors[0] + factors[1] * xcoord + factors[2] * ycoord]
    gather x20 -> x0, local copies, waits for them, and re-layouts: 23.3 us -> none  [basis_step(): lax.dynamic_slice_in_dim(colpass, first_row, window_rows, 0)]
    slice x22 -> x0, local copies, waits for them, and re-layouts: 13.6 us -> none  [the longest x20 12.1 us: poly_field(): factors[0] + factors[1] * xcoord + factors[2] * ycoord]
    ppermute x2 -> x0, starting transfers between devices: 6.22 us -> none  [the longest x1 4.93 us: extended_2(): before = lax.ppermute(last, axis, up)]
  transfers between devices with their start and end apart: 4 -> 0, of which waited for: 2 -> 0; matrix products, arithmetic and copies ran while one was open for 3% -> 0% of each run, Pallas kernels for 0% -> 0%
where the time goes in v1:
time: 35.3 us; the launch traced here: 35.1 us
  Pallas kernels  29.2 us (83%)
  local copies, waits for them, and re-layouts  5.21 us (15%)
  between operations  0.68 us (2%)
    pallas_call x1, Pallas kernels, per_device(): pl.pallas_call(functools.partial(kernel, visits, skies), out_shape=(band,...  29.2 us
    unnamed x15, local copies, waits for them, and re-layouts  5.21 us

profile of v1, /device:TPU:0, one launch (start us, length us, event | category | flops | bytes accessed | tf_op | source)
XLA Modules:
  0.0 35.1 jit_solution(1427372026862106740)
XLA Ops:
  0.6 0.0 copy-start.4
  0.6 0.0 copy-start.3
  0.7 0.0 copy-start.5
  0.7 0.8 %copy.9.coef_ref = f32[1,20,6]{2,1,0:T(8,128)S(1)} copy(f32[1,20,6]{1,0,2:T(1,128)} %param.13) | data formatting | bytes 960 | tf_op args[6]
  1.5 0.0 copy-done.4
  1.5 0.0 copy-done.3
  1.5 0.0 copy-done.5
  1.5 0.0 copy-start
  1.5 1.1 %copy-done = s32[1,384,512]{2,1,0:T(8,128)S(1)} copy-done((s32[1,384,512]{2,1,0:T(8,128)S(1)}, s32[1,384,512]{2,1,0:T(8,128)}, u32[]{:S(2)}) %copy-start) | copy-done | bytes 786456
  2.6 0.0 copy-start.1
  2.6 1.0 %copy-done.1 = bf16[1,384,512]{2,1,0:T(8,128)(2,1)S(1)} copy-done((bf16[1,384,512]{2,1,0:T(8,128)(2,1)S(1)}, bf16[1,384,512]{2,1,0:T(8,128)(2,1)}, u32[]{:S(2)}) %copy-start.1) | copy-done | bytes 393240
  3.6 0.0 copy-start.2
  3.6 1.0 %copy-done.2 = bf16[1,384,512]{2,1,0:T(8,128)(2,1)S(1)} copy-done((bf16[1,384,512]{2,1,0:T(8,128)(2,1)S(1)}, bf16[1,384,512]{2,1,0:T(8,128)(2,1)}, u32[]{:S(2)}) %copy-start.2) | copy-done | bytes 393240
  4.6 29.2 %shard_map.86 = (f32[48,512]{1,0:T(8,128)S(1)}, f32[48,512]{1,0:T(8,128)S(1)}) custom-call(bf16[1,384,512]{2,1,0:T(8,128)(2,1)S(1)} %copy-done.1, bf16[1,384,512]{2,1,0:T(8,128)(2,1)S(1)} %copy-done.2, s32[1,384,512]{2,1,0:T(8,128)S(1)} %copy-done, s32[1,4]{1,0:T(1,128)S(1)} %copy-done.5, bf16[20,41]{1,0:T(8,128)(2,1)S(1)} %copy-done.3, ...), custom_call_target="tpu_custom_call" | custom-call | tf_op jit(solution)/shard_map/pallas_call | solution.py:317
  33.8 0.6 %copy.12 = f32[48,512]{1,0:T(8,128)} copy(f32[48,512]{1,0:T(8,128)S(1)} %get-tuple-element.4) | data formatting | bytes 196608
  34.4 0.6 %copy.13 = f32[48,512]{1,0:T(8,128)} copy(f32[48,512]{1,0:T(8,128)S(1)} %get-tuple-element.5) | data formatting | bytes 196608
Async XLA Ops:
  0.6 0.8 %copy-start.4 = (bf16[20,41]{1,0:T(8,128)(2,1)S(1)}, bf16[20,41]{1,0:T(8,128)(2,1)}, u32[]{:S(2)}) copy-start(bf16[20,41]{1,0:T(8,128)(2,1)} %colf_ref.1) | copy-start | bytes 4924
  0.6 0.8 %copy-start.3 = (bf16[20,41]{1,0:T(8,128)(2,1)S(1)}, bf16[20,41]{1,0:T(8,128)(2,1)}, u32[]{:S(2)}) copy-start(bf16[20,41]{1,0:T(8,128)(2,1)} %rowf_ref.1) | copy-start | bytes 4924
  0.7 0.8 %copy-start.5 = (s32[1,4]{1,0:T(1,128)S(1)}, s32[1,4]{1,0:T(1,128)}, u32[]{:S(2)}) copy-start(s32[1,4]{1,0:T(1,128)} %boxes_ref.1) | copy-start | bytes 52
  1.5 1.1 %copy-start = (s32[1,384,512]{2,1,0:T(8,128)S(1)}, s32[1,384,512]{2,1,0:T(8,128)}, u32[]{:S(2)}) copy-start(s32[1,384,512]{2,1,0:T(8,128)} %bits_ref.1) | copy-start | bytes 2359300
  2.6 1.0 %copy-start.1 = (bf16[1,384,512]{2,1,0:T(8,128)(2,1)S(1)}, bf16[1,384,512]{2,1,0:T(8,128)(2,1)}, u32[]{:S(2)}) copy-start(bf16[1,384,512]{2,1,0:T(8,128)(2,1)} %image_ref.1) | copy-start | bytes 1179652
  3.6 1.0 %copy-start.2 = (bf16[1,384,512]{2,1,0:T(8,128)(2,1)S(1)}, bf16[1,384,512]{2,1,0:T(8,128)(2,1)}, u32[]{:S(2)}) copy-start(bf16[1,384,512]{2,1,0:T(8,128)(2,1)} %var_ref.1) | copy-start | bytes 1179652

commit v2 on v1

v2 whole, which is shorter than its diff:
```python
import functools

import jax
import jax.numpy as jnp
from jax import lax
from jax.experimental import pallas as pl
from jax.experimental.pallas import tpu as pltpu
from jax.sharding import PartitionSpec as P

RAD = 20
ROWS_DEV = 48
REJECT = 7
LANES = 128
GROUP = 4
BAND = GROUP * ROWS_DEV
PAD = 32
WIN = BAND + 2 * PAD
UNITS = 2
MESH = pl.DeviceIdType.MESH


def kernel(
    visits,
    skies,
    image_hbm,
    var_hbm,
    bits_hbm,
    boxes_hbm,
    rowf_hbm,
    colf_hbm,
    coef_hbm,
    sums_ref,
    image_ref,
    var_ref,
    bits_ref,
    boxes_ref,
    rowf_ref,
    colf_ref,
    coef_ref,
    halo_l,
    halo_r,
    masked,
    got_var,
    matched,
    got_pix,
    total,
    windows,
    row_mats,
    col_mats,
    pass_a,
    pass_b,
    filt,
    load_sem,
    var_send,
    var_recv,
    pix_send,
    pix_recv,
    halo_send,
    halo_recv,
):
    height, cols = image_ref.shape[1], image_ref.shape[2]
    width = cols * skies
    basis, taps = rowf_ref.shape
    blocks = cols // LANES
    per_unit = blocks // UNITS
    span = per_unit * LANES
    order = list(range(1, blocks - 1)) + [0, blocks - 1]
    groups = visits // GROUP
    v = lax.axis_index("visit")
    z = lax.axis_index("sky")
    my_group = v // GROUP
    has_l = z > 0
    has_r = z < skies - 1

    barrier = pltpu.get_barrier_semaphore()
    for step in range(1, visits):
        pl.semaphore_signal(
            barrier, inc=1, device_id=(lax.rem(v + step, visits), z), device_id_type=MESH
        )

    @pl.when(has_l)
    def _():
        pl.semaphore_signal(barrier, inc=1, device_id=(v, z - 1), device_id_type=MESH)

    @pl.when(has_r)
    def _():
        pl.semaphore_signal(barrier, inc=1, device_id=(v, z + 1), device_id_type=MESH)

    pairs = (
        (boxes_hbm, boxes_ref),
        (var_hbm, var_ref),
        (bits_hbm, bits_ref),
        (rowf_hbm, rowf_ref),
        (colf_hbm, colf_ref),
        (image_hbm, image_ref),
        (coef_hbm, coef_ref),
    )
    loads = [
        pltpu.make_async_copy(src, dst, load_sem.at[n]) for n, (src, dst) in enumerate(pairs)
    ]
    for load in loads:
        load.start()

    for load in loads[:3]:
        load.wait()
    col_first = z * cols
    box = [boxes_ref[0, i] for i in range(4)]
    col_index = col_first + lax.broadcasted_iota(jnp.int32, (ROWS_DEV, cols), 1)
    col_inside = (col_index >= box[2]) & (col_index < box[3])
    row_iota = lax.broadcasted_iota(jnp.int32, (ROWS_DEV, cols), 0)

    def mask_band(band, carry):
        first = pl.multiple_of(band * ROWS_DEV, ROWS_DEV)
        rows = pl.ds(first, ROWS_DEV)
        row_index = first + row_iota
        inside = (row_index >= box[0]) & (row_index < box[1]) & col_inside
        inside = inside & ((bits_ref[0, rows, :] & REJECT) == 0)
        masked[rows, :] = jnp.where(inside, var_ref[0, rows, :].astype(jnp.float32), 0.0).astype(
            jnp.bfloat16
        )
        return carry

    lax.fori_loop(0, visits, mask_band, 0)

    pl.semaphore_wait(barrier, visits - 1 + has_l.astype(jnp.int32) + has_r.astype(jnp.int32))

    def halo_copy(first, dst, send, recv, target):
        return pltpu.make_async_remote_copy(
            src_ref=image_hbm.at[0, :, pl.ds(first, LANES)],
            dst_ref=dst,
            send_sem=halo_send.at[send],
            recv_sem=halo_recv.at[recv],
            device_id=(v, target),
            device_id_type=MESH,
        )

    @pl.when(has_l)
    def _():
        halo_copy(0, halo_r, 0, 1, z - 1).start()

    @pl.when(has_r)
    def _():
        halo_copy(cols - LANES, halo_l, 1, 0, z + 1).start()

    def rows_of(dest):
        return pl.ds(pl.multiple_of(dest * ROWS_DEV, ROWS_DEV), ROWS_DEV)

    def var_copy(dest, source):
        return pltpu.make_async_remote_copy(
            src_ref=masked.at[rows_of(dest), :],
            dst_ref=got_var.at[source],
            send_sem=var_send.at[dest],
            recv_sem=var_recv.at[source],
            device_id=(dest, z),
            device_id_type=MESH,
        )

    def pix_copy(unit, dest, source):
        return pltpu.make_async_remote_copy(
            src_ref=matched.at[unit, rows_of(dest), :],
            dst_ref=got_pix.at[unit, source],
            send_sem=pix_send.at[unit, dest],
            recv_sem=pix_recv.at[unit, source],
            device_id=(dest, z),
            device_id_type=MESH,
        )

    for step in range(1, visits):
        dest = lax.rem(v + step, visits)
        var_copy(dest, v).start()

    filt[...] = jnp.zeros_like(filt)
    loads[3].wait()
    loads[4].wait()
    filt[0, 0:basis, 0:taps] = rowf_ref[...].astype(jnp.float32)
    filt[1, 0:basis, 0:taps] = colf_ref[...].astype(jnp.float32)
    filt[0] = pltpu.roll(filt[0], PAD - RAD, 1)

    def build(b):
        row = jnp.broadcast_to(filt[0, pl.ds(b, 1), :], (BAND, WIN))
        row_mats[b] = pltpu.roll(row, 0, 1, stride=1, stride_axis=0).astype(jnp.bfloat16)
        col = jnp.broadcast_to(filt[1, pl.ds(b, 1), :], (LANES, 2 * LANES))
        col_mats[b] = pltpu.roll(col, 0, 1, stride=1, stride_axis=0).astype(jnp.bfloat16)

    for k in range(blocks):
        windows[k, 0:PAD, :] = jnp.zeros((PAD, 2 * LANES), jnp.bfloat16)
        windows[k, PAD + height : PAD + height + PAD, :] = jnp.zeros((PAD, 2 * LANES), jnp.bfloat16)

    def shifted(parts, lanes):
        wide = jnp.concatenate(parts, axis=1).astype(jnp.float32)
        back = wide.shape[1] - (LANES - RAD)
        return pltpu.roll(wide, back, 1)[:, :lanes].astype(jnp.bfloat16)

    def window_rows(first):
        return pl.ds(pl.multiple_of(first + PAD, 16), ROWS_DEV)

    def inner_band(band, carry):
        first = pl.multiple_of(band * ROWS_DEV, ROWS_DEV)
        wide = shifted([image_ref[0, pl.ds(first, ROWS_DEV), :]], cols - LANES)
        for k in range(blocks - 2):
            windows[k, window_rows(first), :] = wide[:, k * LANES : (k + 2) * LANES]
        return carry

    def outer_band(band, carry):
        first = pl.multiple_of(band * ROWS_DEV, ROWS_DEV)
        rows = pl.ds(first, ROWS_DEV)
        left = shifted([halo_l[rows, :], image_ref[0, rows, 0 : 2 * LANES]], 2 * LANES)
        windows[blocks - 2, window_rows(first), :] = left
        right = shifted([image_ref[0, rows, cols - 2 * LANES : cols], halo_r[rows, :]], 2 * LANES)
        windows[blocks - 1, window_rows(first), :] = right
        return carry

    loads[5].wait()
    loads[6].wait()
    lax.fori_loop(0, visits, inner_band, 0)

    lane = lax.broadcasted_iota(jnp.int32, (1, LANES), 1)
    y_iota = lax.broadcasted_iota(jnp.int32, (BAND, LANES), 0)

    def one_unit(unit, group, prepare=False):
        first = pl.multiple_of(group * BAND, BAND)
        yc = (2.0 * (first + y_iota).astype(jnp.float32) + 1.0) / height - 1.0
        mine = order[unit * per_unit : (unit + 1) * per_unit]
        xs = []
        for k in mine:
            col_pos = (col_first + k * LANES + lane).astype(jnp.float32)
            xs.append((2.0 * col_pos + 1.0) / width - 1.0)
        total[unit] = jnp.zeros((BAND, span), jnp.float32)

        def col_step(p, passed):
            image_win = windows[unit * per_unit : (unit + 1) * per_unit, pl.ds(first, WIN), :]
            mats = col_mats[pl.ds(2 * p, 2)].reshape(2 * LANES, 2 * LANES)
            out = lax.dot_general(
                image_win.reshape(per_unit * WIN, 2 * LANES),
                mats,
                (((1,), (1,)), ((), ())),
                preferred_element_type=jnp.float32,
            ).astype(jnp.bfloat16)
            for k in range(per_unit):
                for h in range(2):
                    passed[h, :, k * LANES : (k + 1) * LANES] = out[
                        k * WIN : (k + 1) * WIN, h * LANES : (h + 1) * LANES
                    ]

        def row_step(p, passed):
            parts = []
            for h in range(2):
                b = 2 * p + h
                rowpass = jnp.dot(row_mats[b], passed[h], preferred_element_type=jnp.float32)
                parts.append((rowpass, [coef_ref[t, 0, b] for t in range(6)]))
            for k in range(per_unit):
                lanes = slice(k * LANES, (k + 1) * LANES)
                add = total[unit, :, lanes]
                for rowpass, c in parts:
                    in_x = c[0] + c[1] * xs[k] + c[3] * (xs[k] * xs[k])
                    field = in_x + yc * ((c[2] + c[4] * xs[k]) + c[5] * yc)
                    add = add + field * rowpass[:, lanes]
                total[unit, :, lanes] = add

        buffers = (pass_a, pass_b)
        last = basis // 2 - 1
        if prepare:
            build(0)
            build(1)
        col_step(0, buffers[0])
        for p in range(last + 1):
            if prepare and p < last:
                build(2 * p + 2)
                build(2 * p + 3)
            if p < last:
                col_step(p + 1, buffers[(p + 1) % 2])
            row_step(p, buffers[p % 2])
        matched[unit, pl.ds(first, BAND), :] = total[unit].astype(jnp.bfloat16)
        for j in range(GROUP):
            dest = group * GROUP + j

            @pl.when(dest != v)
            def _():
                pix_copy(unit, dest, v).start()

    def group_at(step):
        return lax.rem(my_group + 1 + step, groups)

    one_unit(0, group_at(0), True)

    @pl.when(has_l)
    def _():
        halo_copy(0, halo_l, 0, 0, z - 1).wait_recv()

    @pl.when(has_r)
    def _():
        halo_copy(0, halo_r, 1, 1, z + 1).wait_recv()

    @pl.when(jnp.logical_not(has_l))
    def _():
        halo_l[...] = jnp.zeros_like(halo_l)

    @pl.when(jnp.logical_not(has_r))
    def _():
        halo_r[...] = jnp.zeros_like(halo_r)

    lax.fori_loop(0, visits, outer_band, 0)
    one_unit(1, group_at(0))

    def one_group(step, carry):
        for unit in range(UNITS):
            one_unit(unit, group_at(step))
        return carry

    lax.fori_loop(1, groups, one_group, 0)

    def weight_of(plane):
        plane = plane.astype(jnp.float32)
        positive = plane > 0
        return jnp.where(positive, 1.0 / jnp.where(positive, plane, 1.0), 0.0)

    own_first = pl.multiple_of((v - my_group * GROUP) * ROWS_DEV, ROWS_DEV)
    own_weight = weight_of(masked[rows_of(v), :])
    sums_ref[1] = own_weight

    def in_order(plane_of):
        lanes_of = {}
        for n, k in enumerate(order):
            part = plane_of(n // per_unit)
            at = n % per_unit * LANES
            lanes_of[k] = part[:, at : at + LANES]
        return jnp.concatenate([lanes_of[k] for k in range(blocks)], axis=1)

    sums_ref[0] = own_weight * in_order(lambda unit: total[unit, pl.ds(own_first, ROWS_DEV), :])

    def add_weight(step, carry):
        source = lax.rem(v + step, visits)
        var_copy(source, source).wait_recv()
        sums_ref[1] += weight_of(got_var[source])
        return carry

    lax.fori_loop(1, visits, add_weight, 0)

    base = my_group * GROUP

    def add_source(source):
        for unit in range(UNITS):
            pix_copy(unit, source, source).wait_recv()
        pixels = in_order(lambda unit: got_pix[unit, source]).astype(jnp.float32)
        sums_ref[0] += weight_of(got_var[source]) * pixels

    def add_far(step, carry):
        add_source(lax.rem(base + GROUP + step, visits))
        return carry

    def add_near(step, carry):
        add_source(base + lax.rem(v - base + step, GROUP))
        return carry

    lax.fori_loop(0, visits - GROUP, add_far, 0)
    lax.fori_loop(1, GROUP, add_near, 0)

    for step in range(1, visits):
        dest = lax.rem(v + step, visits)
        var_copy(dest, v).wait_send()
        for unit in range(UNITS):
            pix_copy(unit, dest, v).wait_send()

    @pl.when(has_l)
    def _():
        halo_copy(0, halo_r, 0, 1, z - 1).wait_send()

    @pl.when(has_r)
    def _():
        halo_copy(cols - LANES, halo_l, 1, 0, z + 1).wait_send()


def per_device(image, variance, mask_bits, boxes, row_filters, col_filters, coeffs):
    height, cols = image.shape[1], image.shape[2]
    visits, skies = lax.axis_size("visit"), lax.axis_size("sky")
    basis = row_filters.shape[0]
    blocks = cols // LANES
    span = cols // UNITS
    coeffs = jnp.transpose(coeffs, (2, 0, 1))
    hbm = pl.BlockSpec(memory_space=pltpu.HBM)
    f32, bf16 = jnp.float32, jnp.bfloat16
    dma = pltpu.SemaphoreType.DMA
    sums = pl.pallas_call(
        functools.partial(kernel, visits, skies),
        out_shape=jax.ShapeDtypeStruct((2, ROWS_DEV, cols), f32),
        in_specs=[hbm] * 7,
        out_specs=pl.BlockSpec(memory_space=pltpu.VMEM),
        scratch_shapes=[
            pltpu.VMEM(image.shape, bf16),
            pltpu.VMEM(variance.shape, bf16),
            pltpu.VMEM(mask_bits.shape, jnp.int32),
            pltpu.SMEM(boxes.shape, jnp.int32),
            pltpu.VMEM(row_filters.shape, bf16),
            pltpu.VMEM(col_filters.shape, bf16),
            pltpu.SMEM(coeffs.shape, f32),
            pltpu.VMEM((height, LANES), bf16),
            pltpu.VMEM((height, LANES), bf16),
            pltpu.VMEM((height, cols), bf16),
            pltpu.VMEM((visits, ROWS_DEV, cols), bf16),
            pltpu.VMEM((UNITS, height, span), bf16),
            pltpu.VMEM((UNITS, visits, ROWS_DEV, span), bf16),
            pltpu.VMEM((UNITS, BAND, span), f32),
            pltpu.VMEM((blocks, height + 2 * PAD, 2 * LANES), bf16),
            pltpu.VMEM((basis, BAND, WIN), bf16),
            pltpu.VMEM((basis, LANES, 2 * LANES), bf16),
            pltpu.VMEM((2, WIN, span), bf16),
            pltpu.VMEM((2, WIN, span), bf16),
            pltpu.VMEM((2, 24, WIN), f32),
            dma((7,)),
            dma((visits,)),
            dma((visits,)),
            dma((UNITS, visits)),
            dma((UNITS, visits)),
            dma((2,)),
            dma((2,)),
        ],
        compiler_params=pltpu.CompilerParams(
            collective_id=0, has_side_effects=True, vmem_limit_bytes=62 * 1024 * 1024
        ),
    )(image, variance, mask_bits, boxes, row_filters, col_filters, coeffs)
    return (sums[0] / jnp.maximum(sums[1], 1.0), sums[1])


def solution(mesh):
    in_specs = (
        P("visit", None, "sky"),
        P("visit", None, "sky"),
        P("visit", None, "sky"),
        P("visit", None),
        P(),
        P(),
        P("visit", None, None),
    )
    out_specs = (P("visit", "sky"), P("visit", "sky"))
    return jax.shard_map(
        per_device, mesh=mesh, in_specs=in_specs, out_specs=out_specs, check_vma=False
    )
```

time: 35.3 us -> 23.1 us (0.65)
  Pallas kernels: 29.2 us -> 20.7 us
  local copies, waits for them, and re-layouts: 5.21 us -> 0 us
  other arithmetic: 0 us -> 1.62 us
    pallas_call x1, Pallas kernels: 29.2 us -> 20.7 us  [per_device(): pl.pallas_call(functools.partial(kernel, visits, skies), out_shape=jax.Sh...]
    unnamed x15 -> x0, local copies, waits for them, and re-layouts: 5.21 us -> none
    div x0 -> x1, other arithmetic: none -> 1.62 us  [per_device(): return (sums[0] / jnp.maximum(sums[1], 1.0), sums[1])]
where the time goes in v2:
time: 23.1 us; the launch traced here: 23 us
  Pallas kernels  20.7 us (90%)
  other arithmetic  1.62 us (7%)
  between operations  0.64 us (3%)
    pallas_call x1, Pallas kernels, per_device(): pl.pallas_call(functools.partial(kernel, visits, skies), out_shape=jax.Sh...  20.7 us
    div x1, other arithmetic, per_device(): return (sums[0] / jnp.maximum(sums[1], 1.0), sums[1])  1.62 us

profile of v2, /device:TPU:0, one launch (start us, length us, event | category | flops | bytes accessed | tf_op | source)
XLA Modules:
  0.0 23.0 jit_solution(5196189922786191653)
XLA Ops:
  0.6 20.7 %shard_map.86 = f32[2,48,512]{2,1,0:T(8,128)} custom-call(bf16[1,384,512]{2,1,0:T(8,128)(2,1)} %image_hbm.1, bf16[1,384,512]{2,1,0:T(8,128)(2,1)} %var_hbm.1, s32[1,384,512]{2,1,0:T(8,128)} %bits_hbm.1, s32[1,4]{1,0:T(1,128)} %boxes_hbm.1, bf16[20,41]{1,0:T(8,128)(2,1)} %rowf_hbm.1, bf16[20,41]{1,0:T(8,128)(2,1)} %colf_hbm.1, f32[6,1,20]{2,1,0:T(1,128)} %bitcast.6), custom_call_target="tpu_custom_call" | custom-call | tf_op jit(solution)/shard_map/pallas_call | solution.py:383
  21.3 1.6 %bitcast_divide_fusion = (f32[48,512]{1,0:T(8,128)}, f32[48,512]{1,0:T(8,128)}) fusion(f32[2,48,512]{2,1,0:T(8,128)} %shard_map.86), kind=kLoop, calls=%fused_computation | loop fusion | flops 49152 | bytes 393216 | tf_op jit(solution)/shard_map/div | solution.py:421

commit v3 on v2

--- a/solution.py
+++ b/solution.py
@@ -66,6 +66,7 @@
     span = per_unit * LANES
     order = list(range(1, blocks - 1)) + [0, blocks - 1]
     groups = visits // GROUP
+    few = visits <= 8
     v = lax.axis_index("visit")
     z = lax.axis_index("sky")
     my_group = v // GROUP
@@ -120,7 +121,7 @@
         )
         return carry
 
-    lax.fori_loop(0, visits, mask_band, 0)
+    lax.fori_loop(0, visits, mask_band, 0, unroll=few)
 
     pl.semaphore_wait(barrier, visits - 1 + has_l.astype(jnp.int32) + has_r.astype(jnp.int32))
 
@@ -212,7 +213,7 @@
 
     loads[5].wait()
     loads[6].wait()
-    lax.fori_loop(0, visits, inner_band, 0)
+    lax.fori_loop(0, visits, inner_band, 0, unroll=few)
 
     lane = lax.broadcasted_iota(jnp.int32, (1, LANES), 1)
     y_iota = lax.broadcasted_iota(jnp.int32, (BAND, LANES), 0)
@@ -225,7 +226,6 @@
         for k in mine:
             col_pos = (col_first + k * LANES + lane).astype(jnp.float32)
             xs.append((2.0 * col_pos + 1.0) / width - 1.0)
-        total[unit] = jnp.zeros((BAND, span), jnp.float32)
 
         def col_step(p, passed):
             image_win = windows[unit * per_unit : (unit + 1) * per_unit, pl.ds(first, WIN), :]
@@ -250,7 +250,7 @@
                 parts.append((rowpass, [coef_ref[t, 0, b] for t in range(6)]))
             for k in range(per_unit):
                 lanes = slice(k * LANES, (k + 1) * LANES)
-                add = total[unit, :, lanes]
+                add = 0.0 if p == 0 else total[unit, :, lanes]
                 for rowpass, c in parts:
                     in_x = c[0] + c[1] * xs[k] + c[3] * (xs[k] * xs[k])
                     field = in_x + yc * ((c[2] + c[4] * xs[k]) + c[5] * yc)
@@ -299,7 +299,7 @@
     def _():
         halo_r[...] = jnp.zeros_like(halo_r)
 
-    lax.fori_loop(0, visits, outer_band, 0)
+    lax.fori_loop(0, visits, outer_band, 0, unroll=few)
     one_unit(1, group_at(0))
 
     def one_group(step, carry):
@@ -334,7 +334,7 @@
         sums_ref[1] += weight_of(got_var[source])
         return carry
 
-    lax.fori_loop(1, visits, add_weight, 0)
+    lax.fori_loop(1, visits, add_weight, 0, unroll=few)
 
     base = my_group * GROUP
 
@@ -352,8 +352,8 @@
         add_source(base + lax.rem(v - base + step, GROUP))
         return carry
 
-    lax.fori_loop(0, visits - GROUP, add_far, 0)
-    lax.fori_loop(1, GROUP, add_near, 0)
+    lax.fori_loop(0, visits - GROUP, add_far, 0, unroll=few)
+    lax.fori_loop(1, GROUP, add_near, 0, unroll=few)
 
     for step in range(1, visits):
         dest = lax.rem(v + step, visits)

time: 23.1 us -> 22.5 us (0.974)
  Pallas kernels: 20.7 us -> 20.1 us
    pallas_call x1, Pallas kernels: 20.7 us -> 20.1 us  [per_device(): pl.pallas_call(functools.partial(kernel, visits, skies), out_shape=jax.Sh...]
where the time goes in v3:
time: 22.5 us; the launch traced here: 22.4 us
  Pallas kernels  20.1 us (89%)
  other arithmetic  1.62 us (7%)
  between operations  0.64 us (3%)
    pallas_call x1, Pallas kernels, per_device(): pl.pallas_call(functools.partial(kernel, visits, skies), out_shape=jax.Sh...  20.1 us
    div x1, other arithmetic, per_device(): return (sums[0] / jnp.maximum(sums[1], 1.0), sums[1])  1.62 us

profile of v3, /device:TPU:0, one launch (start us, length us, event | category | flops | bytes accessed | tf_op | source)
XLA Modules:
  0.0 22.4 jit_solution(12225519640197390253)
XLA Ops:
  0.6 20.1 %shard_map.86 = f32[2,48,512]{2,1,0:T(8,128)} custom-call(bf16[1,384,512]{2,1,0:T(8,128)(2,1)} %image_hbm.1, bf16[1,384,512]{2,1,0:T(8,128)(2,1)} %var_hbm.1, s32[1,384,512]{2,1,0:T(8,128)} %bits_hbm.1, s32[1,4]{1,0:T(1,128)} %boxes_hbm.1, bf16[20,41]{1,0:T(8,128)(2,1)} %rowf_hbm.1, bf16[20,41]{1,0:T(8,128)(2,1)} %colf_hbm.1, f32[6,1,20]{2,1,0:T(1,128)} %bitcast.6), custom_call_target="tpu_custom_call" | custom-call | tf_op jit(solution)/shard_map/pallas_call | solution.py:383
  20.8 1.6 %bitcast_divide_fusion = (f32[48,512]{1,0:T(8,128)}, f32[48,512]{1,0:T(8,128)}) fusion(f32[2,48,512]{2,1,0:T(8,128)} %shard_map.86), kind=kLoop, calls=%fused_computation | loop fusion | flops 49152 | bytes 393216 | tf_op jit(solution)/shard_map/div | solution.py:421
